TPU v7x, 512 devices: a whole 4x8x8 slice. The times are simulated.
512 devices in a mesh: sub: 64 (over x, y, core), sep: 8 (over z).
Axes of the slice: x: 4, y: 8, z: 8, core: 2. Of those that a mesh axis runs over, the one named last changes fastest.
Arguments:
- sep_in: float32 [64, 4, 8, 32768], P('sub', None, None, 'sep'), may hold values from -6 to 6
- inv_blocks: bfloat16 [64, 64, 64, 1024], P('sub', None, None, 'sep'), may hold values from -0.75 to 0.75
- couple_blocks: bfloat16 [64, 2, 64, 64, 1024], P('sub', None, None, None, 'sep'), may hold values from -0.5 to 0.5
- face_index: int32 [64, 2, 1024], P('sub', None, 'sep'), may hold values from 0 to 4095
- sep_diag: float32 [64, 32, 32768], P('sub', 'sep'), may hold values from 1 to 3
- sep_couple: float32 [4, 2, 64, 64], replicated, may hold values from -0.5 to 0.5
- sep_index: int32 [64, 32, 512, 2], P('sub', 'sep'), may hold values from 0 to 511
Outputs:
- schur_image: float32 [64, 32, 32768], P('sub', 'sep')
All inputs are finite; a program needn't handle non-finite values.
Results may differ from a plain program's by a relative error of at most 0.0015.
Values may be sent and summed in bfloat16 or wider, within the bound.
A program may use at most 64 MiB of HBM per device.

v0:
```python
import jax
import jax.numpy as jnp
from jax import lax
from jax.sharding import PartitionSpec as P

BS = 64
LEV = 4
KI = 2
KS = 2
HC = 8
ZB = 64
NB = 128
ROWS = 32
FBD = 4096


def partner_2(value, axis, distance):
    mask = 2**distance
    pairs = [(source, source ^ mask) for source in range(lax.axis_size(axis))]
    return lax.ppermute(value, axis, pairs)


def pick_row(args):
    blocks, selector = args
    table = (lax.iota(jnp.int32, blocks.shape[0])[:, None] == selector[None, :]).astype(jnp.float32)
    return lax.dot_general(table, blocks, (((0,), (0,)), ((), ())), precision=lax.Precision.HIGHEST)


def local(sep_in, inv_blocks, couple_blocks, face_index, sep_diag, sep_couple, sep_index):
    subdomain = lax.axis_index("sub")
    own_faces = sep_in[0]
    own_rounded = own_faces.astype(jnp.bfloat16)
    sep_rows = own_faces.reshape(ROWS, ZB * BS)
    halves = []
    for bisect in range(LEV):
        partner = partner_2(own_rounded[bisect], "sub", bisect)
        lower_side = subdomain >> bisect & 1 == 0
        low_half = jnp.where(lower_side, own_rounded[bisect], partner)
        high_half = jnp.where(lower_side, partner, own_rounded[bisect])
        halves.append(jnp.concatenate([low_half, high_half], axis=0))
    whole_face = jnp.stack(halves)
    face_blocks = whole_face.reshape(FBD, BS)
    index_flat = face_index[0].reshape(KI * NB)
    table = (lax.iota(jnp.int32, FBD)[:, None] == index_flat[None, :]).astype(jnp.float32)
    picked = lax.dot_general(
        face_blocks,
        table.astype(jnp.bfloat16),
        (((0,), (0,)), ((), ())),
        preferred_element_type=jnp.float32,
    )
    picked = picked.astype(jnp.bfloat16).reshape(BS, KI, NB)
    coupling = couple_blocks[0]
    driven = jnp.einsum(
        "kijb,jkb->ib", coupling, picked, preferred_element_type=jnp.float32
    ).astype(jnp.bfloat16)
    solved = jnp.einsum(
        "ijb,jb->ib", inv_blocks[0], driven, preferred_element_type=jnp.float32
    ).astype(jnp.bfloat16)
    spread = jnp.einsum(
        "kijb,ib->jkb", coupling, solved, preferred_element_type=jnp.float32
    ).reshape(BS, KI * NB)
    summed = lax.dot_general(
        table, spread, (((1,), (1,)), ((), ())), precision=lax.Precision.HIGHEST
    )
    contrib = summed.reshape(LEV, 2 * HC, ZB * BS)
    conds = []
    for bisect in range(LEV):
        lower_side = subdomain >> bisect & 1 == 0
        own_part = jnp.where(lower_side, contrib[bisect, :HC], contrib[bisect, HC:])
        give_part = jnp.where(lower_side, contrib[bisect, HC:], contrib[bisect, :HC])
        received = partner_2(give_part, "sub", bisect)
        conds.append(own_part + received)
    cond_rows = jnp.stack(conds).reshape(ROWS, ZB * BS)
    sep_cols, cond_cols = (
        lax.all_to_all(sep_rows, "sep", split_axis=0, concat_axis=1, tiled=True),
        lax.all_to_all(cond_rows, "sep", split_axis=0, concat_axis=1, tiled=True),
    )
    owned = ROWS // lax.axis_size("sep")
    first_row = lax.axis_index("sep") * owned
    level_rows = (first_row + lax.iota(jnp.int32, owned)) // HC
    level_table = (level_rows[:, None] == lax.iota(jnp.int32, LEV)[None, :]).astype(jnp.float32)
    couple_rows = jnp.einsum(
        "rl,lkij->rkij", level_table, sep_couple, precision=lax.Precision.HIGHEST
    )
    column_blocks = sep_cols.reshape(owned, -1, BS)
    block_count = column_blocks.shape[1]
    selector = sep_index[0].reshape(owned, block_count * KS)
    chosen = lax.map(pick_row, (column_blocks, selector)).reshape(owned, block_count, KS, BS)
    coupled = jnp.einsum("rnkj,rkij->rni", chosen, couple_rows, precision=lax.Precision.HIGHEST)
    result = sep_diag[0] * sep_cols + coupled.reshape(owned, -1) - cond_cols
    return result[None]


def solution(mesh):
    return jax.shard_map(
        local,
        mesh=mesh,
        in_specs=(
            P("sub", None, None, "sep"),
            P("sub", None, None, "sep"),
            P("sub", None, None, None, "sep"),
            P("sub", None, "sep"),
            P("sub", "sep", None),
            P(),
            P("sub", "sep", None, None),
        ),
        out_specs=P("sub", "sep", None),
        check_vma=False,
    )
```

profile of v0, /device:TPU:1, one launch (start us, length us, event | category | flops | bytes accessed | tf_op | source)
XLA Modules:
  0.0 93.5 jit_solution(15927297686215942986)
XLA Ops:
  0.0 0.0 copy-start
  0.0 0.0 copy-start.4
  0.0 0.0 copy-start.2
  0.0 1.2 %convert_element_type.27 = bf16[1,4,8,4096]{3,2,1,0:T(8,128)(2,1)S(1)} convert(f32[1,4,8,4096]{3,2,1,0:T(8,128)} %param.9) | non-fusion elementwise | flops 131072 | bytes 786432 | tf_op jit(solution)/shard_map/convert_element_type | solution.py:32
  1.2 8.8 %collective-permute-start = (bf16[8,4096]{1,0:T(8,128)(2,1)S(1)}, bf16[8,4096]{1,0:T(8,128)(2,1)S(1)}, u32[]{:S(2)}, u32[]{:S(2)}) collective-permute-start(bf16[8,4096]{1,0:T(8,128)(2,1)S(1)} %get-tuple-element.66), channel_id=1, source_target_pairs={{0,8},{8,0},{16,24},{24,16},{32,40},{40,32},{48,56},{56,48},{64,72... | collective-permute-start | bytes 196616 | tf_op jit(solution)/shard_map/ppermute | solution.py:20
  10.0 2.1 %collective-permute-start.3 = (bf16[8,4096]{1,0:T(8,128)(2,1)S(1)}, bf16[8,4096]{1,0:T(8,128)(2,1)S(1)}, u32[]{:S(2)}, u32[]{:S(2)}) collective-permute-start(bf16[8,4096]{1,0:T(8,128)(2,1)S(1)} %get-tuple-element.67), channel_id=1, source_target_pairs={{0,64},{8,72},{16,80},{24,88},{32,96},{40,104},{48,112},{56,120},{... | collective-permute-start | bytes 196616 | tf_op jit(solution)/shard_map/ppermute | solution.py:20
  12.1 2.4 %collective-permute-start.2 = (bf16[8,4096]{1,0:T(8,128)(2,1)S(1)}, bf16[8,4096]{1,0:T(8,128)(2,1)S(1)}, u32[]{:S(2)}, u32[]{:S(2)}) collective-permute-start(bf16[8,4096]{1,0:T(8,128)(2,1)S(1)} %get-tuple-element.68), channel_id=1, source_target_pairs={{0,32},{8,40},{16,48},{24,56},{32,0},{40,8},{48,16},{56,24},{64,96... | collective-permute-start | bytes 196616 | tf_op jit(solution)/shard_map/ppermute | solution.py:20
  14.5 2.3 %collective-permute-start.1 = (bf16[8,4096]{1,0:T(8,128)(2,1)S(1)}, bf16[8,4096]{1,0:T(8,128)(2,1)S(1)}, u32[]{:S(2)}, u32[]{:S(2)}) collective-permute-start(bf16[8,4096]{1,0:T(8,128)(2,1)S(1)} %get-tuple-element.69), channel_id=1, source_target_pairs={{0,16},{8,24},{16,0},{24,8},{32,48},{40,56},{48,32},{56,40},{64,80... | collective-permute-start | bytes 196616 | tf_op jit(solution)/shard_map/ppermute | solution.py:20
  16.8 2.0 %all_to_all.28 = f32[8,4,4096]{2,1,0:T(4,128)} reshape(f32[1,4,8,4096]{3,2,1,0:T(8,128)} %param.9) | data formatting | bytes 1048576 | tf_op jit(solution)/shard_map/all_to_all | solution.py:75
  18.8 10.0 %all-to-all-start = ((f32[8,4,4096]{2,1,0:T(4,128)}), f32[8,4,4096]{2,1,0:T(4,128)}, u32[]{:S(2)}, u32[]{:S(2)}) async-start(f32[8,4,4096]{2,1,0:T(4,128)} %all_to_all.28), calls=%async_computation | async-start | bytes 1048576 | tf_op jit(solution)/shard_map/all_to_all | solution.py:75
  28.9 0.0 copy-done.4
  28.9 0.3 copy.18
  29.1 0.2 copy.20
  29.3 0.0 copy-done.2
  29.3 4.5 %copy.38 = bf16[64,64,128]{0,1,2:T(8,128)(2,1)} copy(bf16[64,64,128]{2,1,0:T(8,128)(2,1)S(1)} %bitcast.125) | data formatting | bytes 2097152 | tf_op jit(solution)/shard_map/squeeze | solution.py:57
  33.8 0.0 collective-permute-done
  33.9 0.0 collective-permute-done.3
  33.9 0.0 collective-permute-done.2
  33.9 0.0 collective-permute-done.1
  33.9 0.0 copy-start.5
  34.0 0.1 pad_maximum_fusion
  34.1 0.0 copy-start.1
  34.1 2.1 %reshape.82 = bf16[4096,64]{1,0:T(8,128)(2,1)} reshape(bf16[4,16,4096]{2,1,0:T(8,128)(2,1)S(1)} %pad_maximum_fusion) | data formatting | bytes 1048576 | tf_op jit(solution)/shard_map/reshape | solution.py:42
  36.2 0.0 copy-done.5
  36.2 1.7 %fusion.16 = bf16[64,256]{1,0:T(8,128)(2,1)S(1)} fusion(bf16[4096,64]{1,0:T(8,128)(2,1)} %reshape.82, s32[256]{0:T(256)S(1)} %bitcast.130), kind=kOutput, calls=%fused_computation.20 | convolution fusion | flops 137379840 | bytes 558080 | tf_op jit(solution)/shard_map/dot_general | solution.py:45
  38.0 0.0 copy-done.1
  38.0 0.6 multiply_reduce_fusion.1
  38.6 0.1 copy.36
  38.7 2.2 %fusion.26 = f32[128,1,64]{2,1,0:T(1,128)S(1)} fusion(bf16[64,64,128]{0,1,2:T(8,128)(2,1)} %copy.38, bf16[64,128,1]{0,1,2:T(8,128)(2,1)S(1)} %bitcast.129), kind=kOutput, calls=%fused_computation.49 | convolution fusion | flops 1048576 | bytes 1097728 | tf_op jit(solution)/shard_map/ijb,jb->ib/dot_general | solution.py:56
  41.0 0.1 copy.51
  41.0 0.5 multiply_reduce_fusion
  41.5 0.1 copy.47
  41.6 1.9 %fusion.7 = f32[4096,64]{1,0:T(8,128)S(1)} fusion(s32[256]{0:T(256)S(1)} %bitcast.131, f32[8,8,2,128]{3,2,1,0:T(2,128)S(1)} %bitcast.126), kind=kOutput, calls=%fused_computation.13 | convolution fusion | flops 806354944 | bytes 1115136 | tf_op jit(solution)/shard_map/dot_general | solution.py:62
  43.5 0.7 reshape.85
  44.1 0.1 select_bitcast_fusion.3
  44.2 3.0 %collective-permute-start.4 = (f32[8,4096]{1,0:T(8,128)S(1)}, f32[8,4096]{1,0:T(8,128)S(1)}, u32[]{:S(2)}, u32[]{:S(2)}) collective-permute-start(f32[8,4096]{1,0:T(8,128)S(1)} %get-tuple-element.48), channel_id=1, source_target_pairs={{0,8},{8,0},{16,24},{24,16},{32,40},{40,32},{48,56},{56,48},{64,72... | collective-permute-start | bytes 393224 | tf_op jit(solution)/shard_map/ppermute | solution.py:20
  47.2 4.4 %collective-permute-start.7 = (f32[8,4096]{1,0:T(8,128)S(1)}, f32[8,4096]{1,0:T(8,128)S(1)}, u32[]{:S(2)}, u32[]{:S(2)}) collective-permute-start(f32[8,4096]{1,0:T(8,128)S(1)} %get-tuple-element.49), channel_id=1, source_target_pairs={{0,64},{8,72},{16,80},{24,88},{32,96},{40,104},{48,112},{56,120},{... | collective-permute-start | bytes 393224 | tf_op jit(solution)/shard_map/ppermute | solution.py:20
  51.7 2.0 %collective-permute-start.6 = (f32[8,4096]{1,0:T(8,128)S(1)}, f32[8,4096]{1,0:T(8,128)S(1)}, u32[]{:S(2)}, u32[]{:S(2)}) collective-permute-start(f32[8,4096]{1,0:T(8,128)S(1)} %get-tuple-element.50), channel_id=1, source_target_pairs={{0,32},{8,40},{16,48},{24,56},{32,0},{40,8},{48,16},{56,24},{64,96... | collective-permute-start | bytes 393224 | tf_op jit(solution)/shard_map/ppermute | solution.py:20
  53.6 2.3 %collective-permute-start.5 = (f32[8,4096]{1,0:T(8,128)S(1)}, f32[8,4096]{1,0:T(8,128)S(1)}, u32[]{:S(2)}, u32[]{:S(2)}) collective-permute-start(f32[8,4096]{1,0:T(8,128)S(1)} %get-tuple-element.51), channel_id=1, source_target_pairs={{0,16},{8,24},{16,0},{24,8},{32,48},{40,56},{48,32},{56,40},{64,80... | collective-permute-start | bytes 393224 | tf_op jit(solution)/shard_map/ppermute | solution.py:20
  55.9 0.0 copy-done
  56.0 1.2 %fusion.18 = f32[4,2,64,64]{3,0,2,1:T(4,128)} fusion(f32[4,2,64,64]{3,2,1,0:T(8,128)S(1)} %copy-done, s32[4]{0:T(128)S(1)} %and_select_fusion), kind=kOutput, calls=%fused_computation.25 | convolution fusion | flops 1572880 | bytes 262160 | tf_op jit(solution)/shard_map/rl,lkij->rkij/dot_general | solution.py:82
  57.2 0.0 collective-permute-done.4
  57.2 3.2 %collective-permute-done.7 = f32[8,4096]{1,0:T(8,128)S(1)} collective-permute-done((f32[8,4096]{1,0:T(8,128)S(1)}, f32[8,4096]{1,0:T(8,128)S(1)}, u32[]{:S(2)}, u32[]{:S(2)}) %collective-permute-start.7) | collective-permute-done | bytes 131104 | tf_op jit(solution)/shard_map/ppermute | solution.py:20
  60.4 4.5 %collective-permute-done.6 = f32[8,4096]{1,0:T(8,128)S(1)} collective-permute-done((f32[8,4096]{1,0:T(8,128)S(1)}, f32[8,4096]{1,0:T(8,128)S(1)}, u32[]{:S(2)}, u32[]{:S(2)}) %collective-permute-start.6) | collective-permute-done | bytes 131104 | tf_op jit(solution)/shard_map/ppermute | solution.py:20
  64.9 0.0 collective-permute-done.5
  64.9 0.1 fusion.23
  65.0 0.9 %all_to_all.32 = f32[8,4,4096]{2,1,0:T(4,128)} reshape(f32[4,8,4096]{2,1,0:T(8,128)S(1)} %pad_maximum_fusion.1) | data formatting | bytes 1048576 | tf_op jit(solution)/shard_map/all_to_all | solution.py:76
  66.0 0.0 copy-start.3
  66.0 0.0 all-to-all-done
  66.0 7.1 %all-to-all-start.1 = ((f32[8,4,4096]{2,1,0:T(4,128)}), f32[8,4,4096]{2,1,0:T(4,128)}, u32[]{:S(2)}, u32[]{:S(2)}) async-start(f32[8,4,4096]{2,1,0:T(4,128)} %all_to_all.32), calls=%async_computation.1 | async-start | bytes 1048576 | tf_op jit(solution)/shard_map/all_to_all | solution.py:76
  73.0 1.3 %copy.19 = f32[4,8,4096]{2,1,0:T(8,128)S(1)} copy(f32[4,8,4096]{2,0,1:T(4,128)} %bitcast.7) | data formatting | bytes 1048576 | tf_op jit(solution)/shard_map/all_to_all | solution.py:75
  74.4 0.4 reshape.79
  74.8 0.0 copy-done.3
  74.8 3.7 %while.10 = (s32[]{:T(128)}, f32[4,1024,64]{1,2,0:T(8,128)S(1)}, s32[4,1024]{1,0:T(4,128)S(1)}, f32[4,512,64]{2,1,0:T(8,128)S(1)}, s32[]{:T(128)}) while((s32[]{:T(128)}, f32[4,1024,64]{1,2,0:T(8,128)S(1)}, s32[4,1024]{1,0:T(4,128)S(1)}, f32[4,512,64]{2,1,0:T(8,128)S(1)}, s32[]{:T(128)}) %tuple.44), condition=%wide.region_1.2_spmd, body=%wide.region_0.1_spmd.sunk | while | flops 403177472 | bytes 537673 | solution.py:88
  74.8 0.9 fusion.36
  75.8 0.9 fusion.36
  76.7 0.9 fusion.36
  77.6 0.9 fusion.36
  78.5 0.6 copy.21
  79.1 2.9 %fusion.13 = f32[4,512,64]{2,1,0:T(8,128)S(1)} fusion(f32[4,512,2,64]{3,2,1,0:T(2,128)S(1)} %bitcast.123, f32[4,2,64,64]{3,0,2,1:T(4,128)} %fusion.18), kind=kOutput, calls=%fused_computation.19 | convolution fusion | flops 201326592 | bytes 1703936 | tf_op jit(solution)/shard_map/rnkj,rkij->rni/dot_general | solution.py:89
  82.0 0.4 reshape.81
  82.5 8.6 %all-to-all-done.1 = f32[8,4,4096]{2,1,0:T(4,128)} async-done(((f32[8,4,4096]{2,1,0:T(4,128)}), f32[8,4,4096]{2,1,0:T(4,128)}, u32[]{:S(2)}, u32[]{:S(2)}) %all-to-all-start.1) | async-done | bytes 524320 | tf_op jit(solution)/shard_map/all_to_all | solution.py:76
  91.1 2.4 %add_subtract_fusion = f32[1,4,32768]{2,1,0:T(4,128)} fusion(f32[1,4,32768]{2,1,0:T(4,128)} %bitcast.47, f32[1,4,32768]{2,1,0:T(4,128)S(1)} %reshape.81, f32[1,4,32768]{2,1,0:T(4,128)} %param.13, f32[1,4,32768]{2,1,0:T(4,128)} %bitcast.8), kind=kLoop, calls=%fused_computation.23 | loop fusion | flops 393216 | bytes 2621440 | tf_op jit(solution)/shard_map/sub | solution.py:90
  (15 shorter events, 0.2 us)
Async XLA Ops:
  0.0 55.9 %copy-start = (f32[4,2,64,64]{3,2,1,0:T(8,128)S(1)}, f32[4,2,64,64]{3,2,1,0:T(8,128)}, u32[]{:S(2)}) copy-start(f32[4,2,64,64]{3,2,1,0:T(8,128)} %param.14) | copy-start | bytes 393220
  0.0 28.9 %copy-start.4 = (s32[1,4,512,2]{2,3,1,0:T(2,128)S(1)}, s32[1,4,512,2]{2,3,1,0:T(2,128)}, u32[]{:S(2)}) copy-start(s32[1,4,512,2]{2,3,1,0:T(2,128)} %param.15) | copy-start | bytes 49156
  0.0 29.3 %copy-start.2 = (bf16[1,64,64,128]{3,2,1,0:T(8,128)(2,1)S(1)}, bf16[1,64,64,128]{3,2,1,0:T(8,128)(2,1)}, u32[]{:S(2)}) copy-start(bf16[1,64,64,128]{3,2,1,0:T(8,128)(2,1)} %param.10) | copy-start | bytes 3145732
  1.2 32.6 %collective-permute-start = (bf16[8,4096]{1,0:T(8,128)(2,1)S(1)}, bf16[8,4096]{1,0:T(8,128)(2,1)S(1)}, u32[]{:S(2)}, u32[]{:S(2)}) collective-permute-start(bf16[8,4096]{1,0:T(8,128)(2,1)S(1)} %get-tuple-element.66), channel_id=1, source_target_pairs={{0,8},{8,0},{16,24},{24,16},{32,40},{40,32},{48,56},{56,48},{64,72... | collective-permute-start | bytes 196616 | tf_op jit(solution)/shard_map/ppermute | solution.py:20
  10.0 23.9 %collective-permute-start.3 = (bf16[8,4096]{1,0:T(8,128)(2,1)S(1)}, bf16[8,4096]{1,0:T(8,128)(2,1)S(1)}, u32[]{:S(2)}, u32[]{:S(2)}) collective-permute-start(bf16[8,4096]{1,0:T(8,128)(2,1)S(1)} %get-tuple-element.67), channel_id=1, source_target_pairs={{0,64},{8,72},{16,80},{24,88},{32,96},{40,104},{48,112},{56,120},{... | collective-permute-start | bytes 196616 | tf_op jit(solution)/shard_map/ppermute | solution.py:20
  12.1 21.8 %collective-permute-start.2 = (bf16[8,4096]{1,0:T(8,128)(2,1)S(1)}, bf16[8,4096]{1,0:T(8,128)(2,1)S(1)}, u32[]{:S(2)}, u32[]{:S(2)}) collective-permute-start(bf16[8,4096]{1,0:T(8,128)(2,1)S(1)} %get-tuple-element.68), channel_id=1, source_target_pairs={{0,32},{8,40},{16,48},{24,56},{32,0},{40,8},{48,16},{56,24},{64,96... | collective-permute-start | bytes 196616 | tf_op jit(solution)/shard_map/ppermute | solution.py:20
  14.5 19.4 %collective-permute-start.1 = (bf16[8,4096]{1,0:T(8,128)(2,1)S(1)}, bf16[8,4096]{1,0:T(8,128)(2,1)S(1)}, u32[]{:S(2)}, u32[]{:S(2)}) collective-permute-start(bf16[8,4096]{1,0:T(8,128)(2,1)S(1)} %get-tuple-element.69), channel_id=1, source_target_pairs={{0,16},{8,24},{16,0},{24,8},{32,48},{40,56},{48,32},{56,40},{64,80... | collective-permute-start | bytes 196616 | tf_op jit(solution)/shard_map/ppermute | solution.py:20
  18.8 47.1 %all-to-all-start = ((f32[8,4,4096]{2,1,0:T(4,128)}), f32[8,4,4096]{2,1,0:T(4,128)}, u32[]{:S(2)}, u32[]{:S(2)}) async-start(f32[8,4,4096]{2,1,0:T(4,128)} %all_to_all.28), calls=%async_computation | async-start | bytes 1048576 | tf_op jit(solution)/shard_map/all_to_all | solution.py:75
  33.9 2.3 %copy-start.5 = (s32[1,2,128]{2,1,0:T(2,128)S(1)}, s32[1,2,128]{2,1,0:T(2,128)}, u32[]{:S(2)}) copy-start(s32[1,2,128]{2,1,0:T(2,128)} %param.12) | copy-start | bytes 3076
  34.1 3.9 %copy-start.1 = (bf16[1,2,64,64,128]{4,3,2,1,0:T(8,128)(2,1)S(1)}, bf16[1,2,64,64,128]{4,3,2,1,0:T(8,128)(2,1)}, u32[]{:S(2)}) copy-start(bf16[1,2,64,64,128]{4,3,2,1,0:T(8,128)(2,1)} %param.11) | copy-start | bytes 6291460
  44.2 13.0 %collective-permute-start.4 = (f32[8,4096]{1,0:T(8,128)S(1)}, f32[8,4096]{1,0:T(8,128)S(1)}, u32[]{:S(2)}, u32[]{:S(2)}) collective-permute-start(f32[8,4096]{1,0:T(8,128)S(1)} %get-tuple-element.48), channel_id=1, source_target_pairs={{0,8},{8,0},{16,24},{24,16},{32,40},{40,32},{48,56},{56,48},{64,72... | collective-permute-start | bytes 393224 | tf_op jit(solution)/shard_map/ppermute | solution.py:20
  47.2 13.1 %collective-permute-start.7 = (f32[8,4096]{1,0:T(8,128)S(1)}, f32[8,4096]{1,0:T(8,128)S(1)}, u32[]{:S(2)}, u32[]{:S(2)}) collective-permute-start(f32[8,4096]{1,0:T(8,128)S(1)} %get-tuple-element.49), channel_id=1, source_target_pairs={{0,64},{8,72},{16,80},{24,88},{32,96},{40,104},{48,112},{56,120},{... | collective-permute-start | bytes 393224 | tf_op jit(solution)/shard_map/ppermute | solution.py:20
  51.7 13.2 %collective-permute-start.6 = (f32[8,4096]{1,0:T(8,128)S(1)}, f32[8,4096]{1,0:T(8,128)S(1)}, u32[]{:S(2)}, u32[]{:S(2)}) collective-permute-start(f32[8,4096]{1,0:T(8,128)S(1)} %get-tuple-element.50), channel_id=1, source_target_pairs={{0,32},{8,40},{16,48},{24,56},{32,0},{40,8},{48,16},{56,24},{64,96... | collective-permute-start | bytes 393224 | tf_op jit(solution)/shard_map/ppermute | solution.py:20
  53.6 11.2 %collective-permute-start.5 = (f32[8,4096]{1,0:T(8,128)S(1)}, f32[8,4096]{1,0:T(8,128)S(1)}, u32[]{:S(2)}, u32[]{:S(2)}) collective-permute-start(f32[8,4096]{1,0:T(8,128)S(1)} %get-tuple-element.51), channel_id=1, source_target_pairs={{0,16},{8,24},{16,0},{24,8},{32,48},{40,56},{48,32},{56,40},{64,80... | collective-permute-start | bytes 393224 | tf_op jit(solution)/shard_map/ppermute | solution.py:20
  66.0 8.8 %copy-start.3 = (f32[4,1024,64]{1,2,0:T(8,128)S(1)}, f32[4,1024,64]{1,2,0:T(8,128)}, u32[]{:S(2)}) copy-start(f32[4,1024,64]{1,2,0:T(8,128)} %custom-call) | copy-start | bytes 3145732
  66.0 25.1 %all-to-all-start.1 = ((f32[8,4,4096]{2,1,0:T(4,128)}), f32[8,4,4096]{2,1,0:T(4,128)}, u32[]{:S(2)}, u32[]{:S(2)}) async-start(f32[8,4,4096]{2,1,0:T(4,128)} %all_to_all.32), calls=%async_computation.1 | async-start | bytes 1048576 | tf_op jit(solution)/shard_map/all_to_all | solution.py:76
where the time goes:
time: 94.2 us; the launch traced here: 93.5 us
  starting transfers between devices  44.4 us (47%)
  waiting for transfers between devices  16.3 us (17%)
  local copies, waits for them, and re-layouts  13.8 us (15%)
  matrix products  13.6 us (14%)
  other arithmetic  4.97 us (5%)
    ppermute x8, starting transfers between devices, partner_2(): return lax.ppermute(value, axis, pairs)  27.3 us
    all_to_all x1, starting transfers between devices, local(): lax.all_to_all(sep_rows, 'sep', split_axis=0, concat_axis=1, tiled=True)  10 us
    all_to_all x1, waiting for transfers between devices, local(): lax.all_to_all(cond_rows, 'sep', split_axis=0, concat_axis=1, tiled=True)  8.6 us
    ppermute x8, waiting for transfers between devices, partner_2(): return lax.ppermute(value, axis, pairs)  7.72 us
    all_to_all x1, starting transfers between devices, local(): lax.all_to_all(cond_rows, 'sep', split_axis=0, concat_axis=1, tiled=True)  7.05 us
    squeeze x1, local copies, waits for them, and re-layouts, local(): inv_blocks[0]  4.5 us
    dot_general x4, matrix products, pick_row(): lax.dot_general(table, blocks, (((0,), (0,)), ((), ())), precision=lax.Pr...  3.63 us
    all_to_all x2, local copies, waits for them, and re-layouts, local(): lax.all_to_all(sep_rows, 'sep', split_axis=0, concat_axis=1, tiled=True)  3.34 us
  transfers between devices with their start and end apart: 10, of which 3 were waited for; matrix products, arithmetic and copies ran while one was open for 28% of the time, Pallas kernels for 0%

commit v1 on v0

v1 whole, which is shorter than its diff:
```python
import jax
import jax.numpy as jnp
from jax import lax
from jax.experimental import pallas as pl
from jax.experimental.pallas import tpu as pltpu
from jax.sharding import PartitionSpec as P

BS = 64
LEV = 4
NB = 128
NZP = 8
F32 = jnp.float32
BF16 = jnp.bfloat16
MESH = pl.DeviceIdType.MESH
TN = (((0,), (0,)), ((), ()))
NT = (((1,), (1,)), ((), ()))


def one_hot(rows, base, picks):
    place = lax.broadcasted_iota(jnp.int32, (rows, picks.shape[1]), 0) + base
    return jnp.where(place == picks, 1.0, 0.0).astype(BF16)


def halves_by_parity(values, odd):
    return jnp.concatenate([jnp.where(odd, 0.0, values), jnp.where(odd, values, 0.0)], axis=0)


def split(values):
    high = values.astype(BF16)
    return high, (values - high.astype(F32)).astype(BF16)


def kernel(
    sep_hbm, inv_hbm, couple_hbm, fidx_hbm, diag_hbm, w_hbm, sidx_hbm, out_hbm,
    sep_v, inv_v, couple_v, fidx_v, diag_v, w_v, sidx_v, out_v,
    rows_v, face_v, zrows_v, fidx_r, spread_s, spread_r, cond_v, cond_s, cond_r,
    driven_v, solved_v, sidx_t,
    in_sem, out_sem, a_send, a_recv, i_send, i_recv, z_send, z_recv, c_send, c_recv, e_send, e_recv,
):
    s = lax.axis_index("sub")
    z = lax.axis_index("sep")
    side = [lax.rem(lax.div(s, 1 << l), 2) for l in range(LEV)]
    partner = [s + (1 - 2 * side[l]) * (1 << l) for l in range(LEV)]
    own_base = [pl.multiple_of(l * 512 + side[l] * 256, 256) for l in range(LEV)]
    far_base = [pl.multiple_of(l * 512 + (1 - side[l]) * 256, 256) for l in range(LEV)]
    peers = [lax.rem(z + d, NZP) for d in (4, 3, 5, 2, 6, 1, 7)]

    def local(i, src, dst):
        return pltpu.make_async_copy(src, dst, in_sem.at[i])

    loads = [
        local(0, sep_hbm, sep_v),
        local(1, fidx_hbm, fidx_v),
        local(2, couple_hbm, couple_v),
        local(3, inv_hbm, inv_v),
        local(4, sidx_hbm, sidx_v),
        local(5, w_hbm.at[lax.div(z, 2)], w_v),
        local(6, diag_hbm, diag_v),
    ]
    for load in loads:
        load.start()

    barrier = pltpu.get_barrier_semaphore()
    for l in range(LEV):
        pl.semaphore_signal(barrier, inc=1, device_id={"sub": partner[l]}, device_id_type=MESH)
    for peer in peers:
        pl.semaphore_signal(barrier, inc=1, device_id={"sep": peer}, device_id_type=MESH)

    loads[0].wait()
    for l in range(LEV):
        for c in range(8):
            row = sep_v[pl.ds(l * 256 + c, 32, stride=8), :]
            rows_v[pl.ds((l * 8 + c) * 32, 32), :] = row
            face_v[pl.ds(own_base[l] + c * 32, 32), :] = row.astype(BF16)
    loads[1].wait()

    pl.semaphore_wait(barrier, LEV + NZP - 1)

    def to_partner(l, src, dst, send, recv):
        return pltpu.make_async_remote_copy(
            src_ref=src, dst_ref=dst, send_sem=send.at[l], recv_sem=recv.at[l],
            device_id={"sub": partner[l]}, device_id_type=MESH,
        )

    def face_copy(l, base):
        part = face_v.at[pl.ds(base, 256)]
        return to_partner(l, part, part, a_send, a_recv)

    def idx_copy(l):
        return to_partner(l, fidx_v, fidx_r.at[l], i_send, i_recv)

    def spread_copy(l):
        return to_partner(l, spread_s, spread_r.at[l], c_send, c_recv)

    def z_copy(src, dst, slot, place, peer, send, recv, out_slot):
        return pltpu.make_async_remote_copy(
            src_ref=src.at[pl.ds(pl.multiple_of(out_slot * 128, 128), 128)],
            dst_ref=dst.at[pl.ds(pl.multiple_of(place * 128, 128), 128)],
            send_sem=send.at[slot], recv_sem=recv.at[place],
            device_id={"sep": peer}, device_id_type=MESH,
        )

    for l in (3, 2, 1, 0):
        face_copy(l, own_base[l]).start()
    for peer in peers:
        z_copy(rows_v, zrows_v, peer, z, peer, z_send, z_recv, peer).start()
    for l in range(LEV):
        idx_copy(l).start()
    mine = pl.ds(pl.multiple_of(z * 128, 128), 128)
    zrows_v[mine, :] = rows_v[mine, :]

    loads[4].wait()
    block = jnp.concatenate([sidx_v[r] for r in range(4)] * 16, axis=0)
    sidx_t[...] = jnp.transpose(lax.rem(block, 2) * 256 + lax.div(block, 2))

    index = jnp.concatenate([fidx_v[0:1, :], fidx_v[1:2, :]], axis=1)
    odd = lax.rem(index, 2) == 1
    place = lax.div(index, 2)

    def picked_from(base):
        part = face_v[pl.ds(base, 256), :]
        return lax.dot_general(part, one_hot(256, base, place), TN, preferred_element_type=F32)

    picked = picked_from(own_base[0])
    for l in range(1, LEV):
        picked += picked_from(own_base[l])
    loads[2].wait()
    loads[3].wait()
    for l in range(LEV):
        face_copy(l, far_base[l]).wait_recv()
        picked += picked_from(far_base[l])
    picked = jnp.where(odd, picked[BS:], picked[:BS])
    first, second = picked[:, :NB], picked[:, NB:]

    def rows_of(i, body):
        return jnp.concatenate([body(i * 8 + e) for e in range(8)], axis=0)

    def drive(i, carry):
        def one(row):
            total = couple_v[0, row].astype(F32) * first + couple_v[1, row].astype(F32) * second
            return jnp.sum(total, axis=0, keepdims=True)
        driven_v[pl.ds(pl.multiple_of(i * 8, 8), 8), :] = rows_of(i, one)
        return carry

    lax.fori_loop(0, 8, drive, 0)
    driven = driven_v[...].astype(BF16).astype(F32)

    def solve(i, carry):
        def one(row):
            return jnp.sum(inv_v[row].astype(F32) * driven, axis=0, keepdims=True)
        solved_v[pl.ds(pl.multiple_of(i * 8, 8), 8), :] = rows_of(i, one).astype(BF16).astype(F32)
        return carry

    lax.fori_loop(0, 8, solve, 0)

    def spread_step(i, carry):
        low, high = carry
        part = solved_v[pl.ds(pl.multiple_of(i * 8, 8), 8), :]
        for e in range(8):
            row = part[e : e + 1, :]
            low += couple_v[0, i * 8 + e].astype(F32) * row
            high += couple_v[1, i * 8 + e].astype(F32) * row
        return low, high

    zero = jnp.zeros((BS, NB), F32)
    low, high = lax.fori_loop(0, 8, spread_step, (zero, zero))
    spread_s[pl.ds(0, BS), :] = low.astype(BF16)
    spread_s[pl.ds(BS, BS), :] = high.astype(BF16)
    for l in (3, 2, 1, 0):
        spread_copy(l).start()

    own_high, own_low = split(halves_by_parity(jnp.concatenate([low, high], axis=1), odd))
    for l in range(LEV):
        table = one_hot(256, own_base[l], place)
        part = lax.dot_general(table, own_high, NT, preferred_element_type=F32)
        part += lax.dot_general(table, own_low, NT, preferred_element_type=F32)
        cond_v[pl.ds(l * 256, 256), :] = part

    def cond_copy(peer, place):
        return z_copy(cond_s, cond_r, peer, place, peer, e_send, e_recv, peer)

    for l in range(LEV):
        idx_copy(l).wait_recv()
        got = jnp.concatenate([fidx_r[l, 0:1, :], fidx_r[l, 1:2, :]], axis=1)
        spread_copy(l).wait_recv()
        values = spread_r[l].astype(F32)
        values = jnp.concatenate([values[:BS], values[BS:]], axis=1)
        values = halves_by_parity(values, lax.rem(got, 2) == 1).astype(BF16)
        table = one_hot(256, own_base[l], lax.div(got, 2))
        part = cond_v[pl.ds(l * 256, 256), :] + lax.dot_general(
            table, values, NT, preferred_element_type=F32
        )
        cond_s[pl.ds(l * 256, 256), :] = part.astype(BF16)
        for h in range(2):
            q = 2 * l + h

            @pl.when(z != q)
            def _():
                z_copy(cond_s, cond_r, q, z, q, e_send, e_recv, q).start()

            @pl.when(z == q)
            def _():
                cond_r[pl.ds(q * 128, 128), :] = cond_s[pl.ds(q * 128, 128), :]

    loads[5].wait()
    loads[6].wait()
    empty = jnp.zeros((BS, BS), F32)
    weights = []
    for j in range(2):
        w = w_v[j]
        left = jnp.concatenate([w, empty], axis=1)
        right = jnp.concatenate([empty, w], axis=1)
        weights += [left, left, right, right]
    w_high, w_low = split(jnp.concatenate(weights, axis=0))
    first_half = lax.broadcasted_iota(jnp.int32, (256, 128), 1) < BS
    column = lax.broadcasted_iota(jnp.int32, (512, 512), 1)
    picks = jnp.concatenate([sidx_t[pl.ds(e, 256, stride=2), :] for e in range(2)], axis=0)

    for peer in peers:
        z_copy(rows_v, zrows_v, peer, peer, peer, z_send, z_recv, peer).wait_recv()
    for r in range(4):
        x = jnp.concatenate([zrows_v[pl.ds(p * 128 + r * 32, 32), :] for p in range(NZP)], axis=0)
        x_high, x_low = split(x)
        y = lax.dot_general(x_high, w_high, NT, preferred_element_type=F32)
        y += lax.dot_general(x_low, w_high, NT, preferred_element_type=F32)
        y += lax.dot_general(x_high, w_low, NT, preferred_element_type=F32)
        total = None
        for j in range(2):
            table = jnp.where(column == picks[:, 2 * r + j : 2 * r + j + 1], 1.0, 0.0).astype(BF16)
            parts = []
            for half in range(2):
                g = 2 * j + half
                y_high, y_low = split(y[:, g * 128 : (g + 1) * 128])
                parts.append(jnp.where(first_half, y_high.astype(F32), y_low.astype(F32)).astype(BF16))
            term = jnp.dot(table, jnp.concatenate(parts, axis=0), preferred_element_type=F32)
            total = term if total is None else total + term
        total = total + pltpu.roll(total, BS, 1)
        coupled = jnp.where(first_half, total[:256], total[256:])
        spot = pl.ds(r, 256, stride=4)
        out_v[spot, :] = diag_v[spot, :] * x + coupled

    def finish(p):
        for r in range(4):
            spot = pl.ds(p * 128 + r, 32, stride=4)
            part = cond_r[pl.ds(pl.multiple_of(p * 128 + r * 32, 32), 32), :]
            out_v[spot, :] = out_v[spot, :] - part.astype(F32)
        chunk = pl.ds(pl.multiple_of(p * 128, 128), 128)
        pltpu.make_async_copy(out_v.at[chunk], out_hbm.at[chunk], out_sem.at[p]).start()

    finish(z)
    for peer in (peers[6], peers[5], peers[4], peers[3], peers[2], peers[1], peers[0]):
        cond_copy(peer, peer).wait_recv()
        finish(peer)

    for l in range(LEV):
        face_copy(l, own_base[l]).wait_send()
        idx_copy(l).wait_send()
        spread_copy(l).wait_send()
    for peer in peers:
        z_copy(rows_v, zrows_v, peer, z, peer, z_send, z_recv, peer).wait_send()
        cond_copy(peer, z).wait_send()
    for p in range(NZP):
        chunk = pl.ds(p * 128, 128)
        pltpu.make_async_copy(out_v.at[chunk], out_hbm.at[chunk], out_sem.at[p]).wait()


def local(sep_in, inv_blocks, couple_blocks, face_index, sep_diag, sep_couple, sep_index):
    sep_tiles = sep_in.reshape(4, 8, 32, 128).transpose(0, 2, 1, 3).reshape(1024, 128)
    diag_tiles = sep_diag.reshape(4, 256, 128).transpose(1, 0, 2).reshape(1024, 128)
    picks = sep_index.reshape(4, 512, 2).transpose(0, 2, 1)
    dma = pltpu.SemaphoreType.DMA
    out = pl.pallas_call(
        kernel,
        out_shape=jax.ShapeDtypeStruct((1024, 128), F32),
        in_specs=[pl.BlockSpec(memory_space=pl.ANY)] * 7,
        out_specs=pl.BlockSpec(memory_space=pl.ANY),
        scratch_shapes=[
            pltpu.VMEM((1024, 128), F32),
            pltpu.VMEM((64, 64, 128), BF16),
            pltpu.VMEM((2, 64, 64, 128), BF16),
            pltpu.VMEM((2, 128), jnp.int32),
            pltpu.VMEM((1024, 128), F32),
            pltpu.VMEM((2, 64, 64), F32),
            pltpu.VMEM((4, 2, 512), jnp.int32),
            pltpu.VMEM((1024, 128), F32),
            pltpu.VMEM((1024, 128), F32),
            pltpu.VMEM((2048, 128), BF16),
            pltpu.VMEM((1024, 128), F32),
            pltpu.VMEM((4, 2, 128), jnp.int32),
            pltpu.VMEM((128, 128), BF16),
            pltpu.VMEM((4, 128, 128), BF16),
            pltpu.VMEM((1024, 128), F32),
            pltpu.VMEM((1024, 128), BF16),
            pltpu.VMEM((1024, 128), BF16),
            pltpu.VMEM((64, 128), F32),
            pltpu.VMEM((64, 128), F32),
            pltpu.VMEM((512, 128), jnp.int32),
            dma((7,)),
            dma((8,)),
            dma((4,)),
            dma((4,)),
            dma((4,)),
            dma((4,)),
            dma((8,)),
            dma((8,)),
            dma((4,)),
            dma((4,)),
            dma((8,)),
            dma((8,)),
        ],
        compiler_params=pltpu.CompilerParams(
            collective_id=0, has_side_effects=True, vmem_limit_bytes=62 * 1024 * 1024
        ),
        cost_estimate=pl.CostEstimate(flops=3_000_000_000, bytes_accessed=5_000_000, transcendentals=0),
    )(
        sep_tiles, inv_blocks.reshape(64, 64, 128), couple_blocks.reshape(2, 64, 64, 128),
        face_index.reshape(2, 128), diag_tiles, sep_couple, picks,
    )
    return out.reshape(256, 4, 128).transpose(1, 0, 2).reshape(1, 4, 32768)


def solution(mesh):
    return jax.shard_map(
        local,
        mesh=mesh,
        in_specs=(
            P("sub", None, None, "sep"),
            P("sub", None, None, "sep"),
            P("sub", None, None, None, "sep"),
            P("sub", None, "sep"),
            P("sub", "sep", None),
            P(),
            P("sub", "sep", None, None),
        ),
        out_specs=P("sub", "sep", None),
        check_vma=False,
    )
```

time: 94.2 us -> 36.4 us (0.39)
  starting transfers between devices: 44.4 us -> 0 us
  Pallas kernels: 0 us -> 34.3 us
  waiting for transfers between devices: 16.3 us -> 0 us
  matrix products: 13.6 us -> 0 us
  local copies, waits for them, and re-layouts: 13.8 us -> 1.87 us
  other arithmetic: 4.97 us -> 0 us
    pallas_call x0 -> x1, Pallas kernels: none -> 34.3 us  [local(): pl.pallas_call(kernel, out_shape=jax.ShapeDtypeStruct((1024, 128), F32),...]
    ppermute x8 -> x0, starting transfers between devices: 27.3 us -> none  [partner_2(): return lax.ppermute(value, axis, pairs)]
    all_to_all x2 -> x0, starting transfers between devices: 17.1 us -> none  [the longest x1 10 us: local(): lax.all_to_all(sep_rows, 'sep', split_axis=0, concat_axis=1, tiled=True)]
    dot_general x9 -> x0, matrix products: 13.6 us -> none  [the longest x4 3.63 us: pick_row(): lax.dot_general(table, blocks, (((0,), (0,)), ((), ())), precision=lax.Pr...]
    all_to_all x2 -> x0, waiting for transfers between devices: 8.61 us -> none  [the longest x1 8.6 us: local(): lax.all_to_all(cond_rows, 'sep', split_axis=0, concat_axis=1, tiled=True)]
    ppermute x8 -> x0, waiting for transfers between devices: 7.72 us -> none  [partner_2(): return lax.ppermute(value, axis, pairs)]
    squeeze x2 -> x0, local copies, waits for them, and re-layouts: 4.52 us -> none  [the longest x1 4.5 us: local(): inv_blocks[0]]
    all_to_all x3 -> x0, local copies, waits for them, and re-layouts: 4.28 us -> none  [the longest x2 3.34 us: local(): lax.all_to_all(sep_rows, 'sep', split_axis=0, concat_axis=1, tiled=True)]
  transfers between devices with their start and end apart: 10 -> 0, of which waited for: 3 -> 0; matrix products, arithmetic and copies ran while one was open for 28% -> 0% of each run, Pallas kernels for 0% -> 0%
where the time goes in v1:
time: 36.4 us; the launch traced here: 36.2 us
  Pallas kernels  34.3 us (94%)
  local copies, waits for them, and re-layouts  1.87 us (5%)
    pallas_call x1, Pallas kernels, local(): pl.pallas_call(kernel, out_shape=jax.ShapeDtypeStruct((1024, 128), F32),...  34.3 us
    unnamed x1, local copies, waits for them, and re-layouts  1.87 us

profile of v1, /device:TPU:1, one launch (start us, length us, event | category | flops | bytes accessed | tf_op | source)
XLA Modules:
  0.0 36.2 jit_solution(9801841048573439854)
XLA Ops:
  0.0 34.3 %shard_map.73 = f32[1024,128]{1,0:T(8,128)} custom-call(f32[1024,128]{1,0:T(8,128)} %bitcast.24, bf16[64,64,128]{2,1,0:T(8,128)(2,1)} %bitcast.23, bf16[2,64,64,128]{3,2,1,0:T(8,128)(2,1)} %bitcast.22, s32[2,128]{1,0:T(2,128)} %bitcast.27, f32[1024,128]{1,0:T(8,128)} %bitcast.25, f32[4,2,64,64]{3,2,1,0:T(8,128)} %w_hbm.1, s32[4,2,512]{2,1,0:T(2,128)} %bitcast.26), custom_call_target="tpu_custom_call" | custom-call | flops 3000000000 | bytes 5000000 | tf_op jit(solution)/shard_map/pallas_call | solution.py:272
  34.3 1.9 %copy.11 = f32[1,4,32768]{2,1,0:T(4,128)} copy(f32[1,4,32768]{2,1,0:T(4,128)} %bitcast.21) | data formatting | bytes 1048576

commit v2 on v1

--- a/solution.py
+++ b/solution.py
@@ -31,18 +31,18 @@
 
 
 def kernel(
-    sep_hbm, inv_hbm, couple_hbm, fidx_hbm, diag_hbm, w_hbm, sidx_hbm, out_hbm,
-    sep_v, inv_v, couple_v, fidx_v, diag_v, w_v, sidx_v, out_v,
-    rows_v, face_v, zrows_v, fidx_r, spread_s, spread_r, cond_v, cond_s, cond_r,
+    sep_hbm, inv_hbm, couple_hbm, fidx_hbm, diag_hbm, w_hbm, sidx_hbm, out_v, cond_r,
+    sep_v, inv_v, couple_v, fidx_v, diag_v, w_v, sidx_v,
+    rows_v, face_v, far_v, zrows_v, fidx_r, pick_s, pick_r, spread_s, spread_r, cond_v, cond_s,
     driven_v, solved_v, sidx_t,
-    in_sem, out_sem, a_send, a_recv, i_send, i_recv, z_send, z_recv, c_send, c_recv, e_send, e_recv,
+    in_sem, a_send, a_recv, i_send, i_recv, z_send, z_recv, c_send, c_recv, e_send, e_recv,
 ):
     s = lax.axis_index("sub")
     z = lax.axis_index("sep")
     side = [lax.rem(lax.div(s, 1 << l), 2) for l in range(LEV)]
     partner = [s + (1 - 2 * side[l]) * (1 << l) for l in range(LEV)]
     own_base = [pl.multiple_of(l * 512 + side[l] * 256, 256) for l in range(LEV)]
-    far_base = [pl.multiple_of(l * 512 + (1 - side[l]) * 256, 256) for l in range(LEV)]
+    far_base = (LEV - 1) * 512 + (1 - side[LEV - 1]) * 256
     peers = [lax.rem(z + d, NZP) for d in (4, 3, 5, 2, 6, 1, 7)]
 
     def local(i, src, dst):
@@ -71,7 +71,7 @@
         for c in range(8):
             row = sep_v[pl.ds(l * 256 + c, 32, stride=8), :]
             rows_v[pl.ds((l * 8 + c) * 32, 32), :] = row
-            face_v[pl.ds(own_base[l] + c * 32, 32), :] = row.astype(BF16)
+            face_v[pl.ds((l * 8 + c) * 32, 32), :] = row.astype(BF16)
     loads[1].wait()
 
     pl.semaphore_wait(barrier, LEV + NZP - 1)
@@ -82,9 +82,11 @@
             device_id={"sub": partner[l]}, device_id_type=MESH,
         )
 
-    def face_copy(l, base):
-        part = face_v.at[pl.ds(base, 256)]
-        return to_partner(l, part, part, a_send, a_recv)
+    def face_copy():
+        return to_partner(LEV - 1, face_v.at[pl.ds((LEV - 1) * 256, 256)], far_v, a_send, a_recv)
+
+    def pick_copy(l):
+        return to_partner(l, pick_s.at[l], pick_r.at[l], a_send, a_recv)
 
     def idx_copy(l):
         return to_partner(l, fidx_v, fidx_r.at[l], i_send, i_recv)
@@ -100,12 +102,11 @@
             device_id={"sep": peer}, device_id_type=MESH,
         )
 
-    for l in (3, 2, 1, 0):
-        face_copy(l, own_base[l]).start()
+    face_copy().start()
+    for l in (2, 1, 0, 3):
+        idx_copy(l).start()
     for peer in peers:
         z_copy(rows_v, zrows_v, peer, z, peer, z_send, z_recv, peer).start()
-    for l in range(LEV):
-        idx_copy(l).start()
     mine = pl.ds(pl.multiple_of(z * 128, 128), 128)
     zrows_v[mine, :] = rows_v[mine, :]
 
@@ -113,23 +114,34 @@
     block = jnp.concatenate([sidx_v[r] for r in range(4)] * 16, axis=0)
     sidx_t[...] = jnp.transpose(lax.rem(block, 2) * 256 + lax.div(block, 2))
 
-    index = jnp.concatenate([fidx_v[0:1, :], fidx_v[1:2, :]], axis=1)
-    odd = lax.rem(index, 2) == 1
-    place = lax.div(index, 2)
-
-    def picked_from(base):
-        part = face_v[pl.ds(base, 256), :]
-        return lax.dot_general(part, one_hot(256, base, place), TN, preferred_element_type=F32)
-
-    picked = picked_from(own_base[0])
+    def places(pair):
+        both = jnp.concatenate([pair[0:1, :], pair[1:2, :]], axis=1)
+        return lax.rem(both, 2) == 1, lax.div(both, 2)
+
+    def picked_from(part, base, at):
+        return lax.dot_general(part, one_hot(256, base, at), TN, preferred_element_type=F32)
+
+    odd, place = places(fidx_v[...])
+    for l in (0, 1, 2):
+        idx_copy(l).wait_recv()
+        got_odd, got_place = places(fidx_r[l])
+        got = picked_from(face_v[pl.ds(l * 256, 256), :], own_base[l], got_place)
+        got = jnp.where(got_odd, got[BS:], got[:BS])
+        pick_s[l] = jnp.concatenate([got[:, :NB], got[:, NB:]], axis=0).astype(BF16)
+        pick_copy(l).start()
+    picked = picked_from(face_v[pl.ds(0, 256), :], own_base[0], place)
     for l in range(1, LEV):
-        picked += picked_from(own_base[l])
+        picked += picked_from(face_v[pl.ds(l * 256, 256), :], own_base[l], place)
     loads[2].wait()
     loads[3].wait()
-    for l in range(LEV):
-        face_copy(l, far_base[l]).wait_recv()
-        picked += picked_from(far_base[l])
+    near = jnp.zeros((2 * BS, NB), F32)
+    for l in (0, 1, 2):
+        pick_copy(l).wait_recv()
+        near += pick_r[l].astype(F32)
+    face_copy().wait_recv()
+    picked += picked_from(far_v[...], far_base, place)
     picked = jnp.where(odd, picked[BS:], picked[:BS])
+    picked += jnp.concatenate([near[:BS], near[BS:]], axis=1)
     first, second = picked[:, :NB], picked[:, NB:]
 
     def rows_of(i, body):
@@ -180,13 +192,14 @@
         return z_copy(cond_s, cond_r, peer, place, peer, e_send, e_recv, peer)
 
     for l in range(LEV):
-        idx_copy(l).wait_recv()
-        got = jnp.concatenate([fidx_r[l, 0:1, :], fidx_r[l, 1:2, :]], axis=1)
+        if l == LEV - 1:
+            idx_copy(l).wait_recv()
+        got_odd, got_place = places(fidx_r[l])
         spread_copy(l).wait_recv()
         values = spread_r[l].astype(F32)
         values = jnp.concatenate([values[:BS], values[BS:]], axis=1)
-        values = halves_by_parity(values, lax.rem(got, 2) == 1).astype(BF16)
-        table = one_hot(256, own_base[l], lax.div(got, 2))
+        values = halves_by_parity(values, got_odd).astype(BF16)
+        table = one_hot(256, own_base[l], got_place)
         part = cond_v[pl.ds(l * 256, 256), :] + lax.dot_general(
             table, values, NT, preferred_element_type=F32
         )
@@ -239,29 +252,28 @@
         spot = pl.ds(r, 256, stride=4)
         out_v[spot, :] = diag_v[spot, :] * x + coupled
 
-    def finish(p):
+    for peer in peers:
+        cond_copy(peer, peer).wait_recv()
+    for l in range(LEV):
+        (face_copy() if l == LEV - 1 else pick_copy(l)).wait_send()
+        idx_copy(l).wait_send()
+        spread_copy(l).wait_send()
+    for peer in peers:
+        z_copy(rows_v, zrows_v, peer, z, peer, z_send, z_recv, peer).wait_send()
+        cond_copy(peer, z).wait_send()
+
+
+def last(part, cond, out_hbm, out_v, sem):
+    copies = []
+    for p in range(NZP):
+        chunk = pl.ds(p * 128, 128)
         for r in range(4):
             spot = pl.ds(p * 128 + r, 32, stride=4)
-            part = cond_r[pl.ds(pl.multiple_of(p * 128 + r * 32, 32), 32), :]
-            out_v[spot, :] = out_v[spot, :] - part.astype(F32)
-        chunk = pl.ds(pl.multiple_of(p * 128, 128), 128)
-        pltpu.make_async_copy(out_v.at[chunk], out_hbm.at[chunk], out_sem.at[p]).start()
-
-    finish(z)
-    for peer in (peers[6], peers[5], peers[4], peers[3], peers[2], peers[1], peers[0]):
-        cond_copy(peer, peer).wait_recv()
-        finish(peer)
-
-    for l in range(LEV):
-        face_copy(l, own_base[l]).wait_send()
-        idx_copy(l).wait_send()
-        spread_copy(l).wait_send()
-    for peer in peers:
-        z_copy(rows_v, zrows_v, peer, z, peer, z_send, z_recv, peer).wait_send()
-        cond_copy(peer, z).wait_send()
-    for p in range(NZP):
-        chunk = pl.ds(p * 128, 128)
-        pltpu.make_async_copy(out_v.at[chunk], out_hbm.at[chunk], out_sem.at[p]).wait()
+            out_v[spot, :] = part[spot, :] - cond[pl.ds(p * 128 + r * 32, 32), :].astype(F32)
+        copies.append(pltpu.make_async_copy(out_v.at[chunk], out_hbm.at[chunk], sem.at[p]))
+        copies[-1].start()
+    for copy in copies:
+        copy.wait()
 
 
 def local(sep_in, inv_blocks, couple_blocks, face_index, sep_diag, sep_couple, sep_index):
@@ -269,11 +281,11 @@
     diag_tiles = sep_diag.reshape(4, 256, 128).transpose(1, 0, 2).reshape(1024, 128)
     picks = sep_index.reshape(4, 512, 2).transpose(0, 2, 1)
     dma = pltpu.SemaphoreType.DMA
-    out = pl.pallas_call(
+    part, cond = pl.pallas_call(
         kernel,
-        out_shape=jax.ShapeDtypeStruct((1024, 128), F32),
+        out_shape=(pltpu.VMEM((1024, 128), F32), pltpu.VMEM((1024, 128), BF16)),
         in_specs=[pl.BlockSpec(memory_space=pl.ANY)] * 7,
-        out_specs=pl.BlockSpec(memory_space=pl.ANY),
+        out_specs=(pl.BlockSpec(memory_space=pltpu.VMEM), pl.BlockSpec(memory_space=pltpu.VMEM)),
         scratch_shapes=[
             pltpu.VMEM((1024, 128), F32),
             pltpu.VMEM((64, 64, 128), BF16),
@@ -283,20 +295,20 @@
             pltpu.VMEM((2, 64, 64), F32),
             pltpu.VMEM((4, 2, 512), jnp.int32),
             pltpu.VMEM((1024, 128), F32),
-            pltpu.VMEM((1024, 128), F32),
-            pltpu.VMEM((2048, 128), BF16),
+            pltpu.VMEM((1024, 128), BF16),
+            pltpu.VMEM((256, 128), BF16),
             pltpu.VMEM((1024, 128), F32),
             pltpu.VMEM((4, 2, 128), jnp.int32),
+            pltpu.VMEM((3, 128, 128), BF16),
+            pltpu.VMEM((3, 128, 128), BF16),
             pltpu.VMEM((128, 128), BF16),
             pltpu.VMEM((4, 128, 128), BF16),
             pltpu.VMEM((1024, 128), F32),
-            pltpu.VMEM((1024, 128), BF16),
             pltpu.VMEM((1024, 128), BF16),
             pltpu.VMEM((64, 128), F32),
             pltpu.VMEM((64, 128), F32),
             pltpu.VMEM((512, 128), jnp.int32),
             dma((7,)),
-            dma((8,)),
             dma((4,)),
             dma((4,)),
             dma((4,)),
@@ -315,6 +327,16 @@
     )(
         sep_tiles, inv_blocks.reshape(64, 64, 128), couple_blocks.reshape(2, 64, 64, 128),
         face_index.reshape(2, 128), diag_tiles, sep_couple, picks,
+    )
+    out = pl.pallas_call(
+        last,
+        out_shape=jax.ShapeDtypeStruct((1024, 128), F32),
+        in_specs=[pl.BlockSpec(memory_space=pltpu.VMEM)] * 2,
+        out_specs=pl.BlockSpec(memory_space=pl.ANY),
+        scratch_shapes=[pltpu.VMEM((1024, 128), F32), dma((8,))],
+    )(
+        pltpu.with_memory_space_constraint(part, pltpu.VMEM),
+        pltpu.with_memory_space_constraint(cond, pltpu.VMEM),
     )
     return out.reshape(256, 4, 128).transpose(1, 0, 2).reshape(1, 4, 32768)
 

time: 36.4 us -> 34 us (0.934)
  local copies, waits for them, and re-layouts: 1.87 us -> 0 us
  Pallas kernels: 34.3 us -> 33.9 us
    unnamed x1 -> x0, local copies, waits for them, and re-layouts: 1.87 us -> none
    pallas_call x1 -> x2, Pallas kernels: 34.3 us -> 33.9 us  [the longest x1 33 us: local(): pl.pallas_call(kernel, out_shape=(pltpu.VMEM((1024, 128), F32), pltpu.VME...]
where the time goes in v2:
time: 34 us; the launch traced here: 33.9 us
  Pallas kernels  33.9 us (100%)
    pallas_call x1, Pallas kernels, local(): pl.pallas_call(kernel, out_shape=(pltpu.VMEM((1024, 128), F32), pltpu.VME...  33 us
    pallas_call x1, Pallas kernels, local(): pl.pallas_call(last, out_shape=jax.ShapeDtypeStruct((1024, 128), F32), in...  0.86 us

profile of v2, /device:TPU:1, one launch (start us, length us, event | category | flops | bytes accessed | tf_op | source)
XLA Modules:
  0.0 33.9 jit_solution(3382891340920898471)
XLA Ops:
  0.0 33.0 %shard_map.73 = (f32[1024,128]{1,0:T(8,128)S(1)}, bf16[1024,128]{1,0:T(8,128)(2,1)S(1)}) custom-call(f32[1024,128]{1,0:T(8,128)} %bitcast.23, bf16[64,64,128]{2,1,0:T(8,128)(2,1)} %bitcast.22, bf16[2,64,64,128]{3,2,1,0:T(8,128)(2,1)} %bitcast.21, s32[2,128]{1,0:T(2,128)} %bitcast.26, f32[1024,128]{1,0:T(8,128)} %bitcast.24, f32[4,2,64,64]{3,2,1,0:T(8,128)} %w_hbm.1, ...), custom_call_target="tpu_custom_call" | custom-call | flops 3000000000 | bytes 5000000 | tf_op jit(solution)/shard_map/pallas_call | solution.py:284
  33.0 0.9 %shard_map.74 = f32[1024,128]{1,0:T(8,128)} custom-call(f32[1024,128]{1,0:T(8,128)S(1)} %get-tuple-element.7.part, bf16[1024,128]{1,0:T(8,128)(2,1)S(1)} %get-tuple-element.8.cond), custom_call_target="tpu_custom_call" | custom-call | tf_op jit(solution)/shard_map/pallas_call | solution.py:331

commit v3 on v2

--- a/solution.py
+++ b/solution.py
@@ -61,7 +61,7 @@
         load.start()
 
     barrier = pltpu.get_barrier_semaphore()
-    for l in range(LEV):
+    for l in (3, 2, 1, 0):
         pl.semaphore_signal(barrier, inc=1, device_id={"sub": partner[l]}, device_id_type=MESH)
     for peer in peers:
         pl.semaphore_signal(barrier, inc=1, device_id={"sep": peer}, device_id_type=MESH)
@@ -102,9 +102,10 @@
             device_id={"sep": peer}, device_id_type=MESH,
         )
 
+    for l in (2, 1, 0):
+        idx_copy(l).start()
     face_copy().start()
-    for l in (2, 1, 0, 3):
-        idx_copy(l).start()
+    idx_copy(LEV - 1).start()
     for peer in peers:
         z_copy(rows_v, zrows_v, peer, z, peer, z_send, z_recv, peer).start()
     mine = pl.ds(pl.multiple_of(z * 128, 128), 128)
@@ -154,7 +155,7 @@
         driven_v[pl.ds(pl.multiple_of(i * 8, 8), 8), :] = rows_of(i, one)
         return carry
 
-    lax.fori_loop(0, 8, drive, 0)
+    lax.fori_loop(0, 8, drive, 0, unroll=2)
     driven = driven_v[...].astype(BF16).astype(F32)
 
     def solve(i, carry):
@@ -163,7 +164,7 @@
         solved_v[pl.ds(pl.multiple_of(i * 8, 8), 8), :] = rows_of(i, one).astype(BF16).astype(F32)
         return carry
 
-    lax.fori_loop(0, 8, solve, 0)
+    lax.fori_loop(0, 8, solve, 0, unroll=2)
 
     def spread_step(i, carry):
         low, high = carry
@@ -175,7 +176,7 @@
         return low, high
 
     zero = jnp.zeros((BS, NB), F32)
-    low, high = lax.fori_loop(0, 8, spread_step, (zero, zero))
+    low, high = lax.fori_loop(0, 8, spread_step, (zero, zero), unroll=2)
     spread_s[pl.ds(0, BS), :] = low.astype(BF16)
     spread_s[pl.ds(BS, BS), :] = high.astype(BF16)
     for l in (3, 2, 1, 0):

time: 34 us -> 34.4 us (1.012)
  Pallas kernels: 33.9 us -> 34.3 us
    pallas_call x1, Pallas kernels: 33 us -> 33.4 us  [local(): pl.pallas_call(kernel, out_shape=(pltpu.VMEM((1024, 128), F32), pltpu.VME...]
where the time goes in v3:
time: 34.4 us; the launch traced here: 34.3 us
  Pallas kernels  34.3 us (100%)
    pallas_call x1, Pallas kernels, local(): pl.pallas_call(kernel, out_shape=(pltpu.VMEM((1024, 128), F32), pltpu.VME...  33.4 us
    pallas_call x1, Pallas kernels, local(): pl.pallas_call(last, out_shape=jax.ShapeDtypeStruct((1024, 128), F32), in...  0.86 us

profile of v3, /device:TPU:1, one launch (start us, length us, event | category | flops | bytes accessed | tf_op | source)
XLA Modules:
  0.0 34.3 jit_solution(11113634029648114906)
XLA Ops:
  0.0 33.4 %shard_map.73 = (f32[1024,128]{1,0:T(8,128)S(1)}, bf16[1024,128]{1,0:T(8,128)(2,1)S(1)}) custom-call(f32[1024,128]{1,0:T(8,128)} %bitcast.23, bf16[64,64,128]{2,1,0:T(8,128)(2,1)} %bitcast.22, bf16[2,64,64,128]{3,2,1,0:T(8,128)(2,1)} %bitcast.21, s32[2,128]{1,0:T(2,128)} %bitcast.26, f32[1024,128]{1,0:T(8,128)} %bitcast.24, f32[4,2,64,64]{3,2,1,0:T(8,128)} %w_hbm.1, ...), custom_call_target="tpu_custom_call" | custom-call | flops 3000000000 | bytes 5000000 | tf_op jit(solution)/shard_map/pallas_call | solution.py:285
  33.4 0.9 %shard_map.74 = f32[1024,128]{1,0:T(8,128)} custom-call(f32[1024,128]{1,0:T(8,128)S(1)} %get-tuple-element.7.part, bf16[1024,128]{1,0:T(8,128)(2,1)S(1)} %get-tuple-element.8.cond), custom_call_target="tpu_custom_call" | custom-call | tf_op jit(solution)/shard_map/pallas_call | solution.py:332

commit v4 on v3

--- a/solution.py
+++ b/solution.py
@@ -61,7 +61,7 @@
         load.start()
 
     barrier = pltpu.get_barrier_semaphore()
-    for l in (3, 2, 1, 0):
+    for l in range(LEV):
         pl.semaphore_signal(barrier, inc=1, device_id={"sub": partner[l]}, device_id_type=MESH)
     for peer in peers:
         pl.semaphore_signal(barrier, inc=1, device_id={"sep": peer}, device_id_type=MESH)
@@ -123,6 +123,11 @@
         return lax.dot_general(part, one_hot(256, base, at), TN, preferred_element_type=F32)
 
     odd, place = places(fidx_v[...])
+    picked = picked_from(face_v[pl.ds(0, 256), :], own_base[0], place)
+    for l in range(1, LEV):
+        picked += picked_from(face_v[pl.ds(l * 256, 256), :], own_base[l], place)
+    loads[2].wait()
+    loads[3].wait()
     for l in (0, 1, 2):
         idx_copy(l).wait_recv()
         got_odd, got_place = places(fidx_r[l])
@@ -130,11 +135,6 @@
         got = jnp.where(got_odd, got[BS:], got[:BS])
         pick_s[l] = jnp.concatenate([got[:, :NB], got[:, NB:]], axis=0).astype(BF16)
         pick_copy(l).start()
-    picked = picked_from(face_v[pl.ds(0, 256), :], own_base[0], place)
-    for l in range(1, LEV):
-        picked += picked_from(face_v[pl.ds(l * 256, 256), :], own_base[l], place)
-    loads[2].wait()
-    loads[3].wait()
     near = jnp.zeros((2 * BS, NB), F32)
     for l in (0, 1, 2):
         pick_copy(l).wait_recv()

time: 34.4 us -> 33.6 us (0.977)
  Pallas kernels: 34.3 us -> 33.5 us
    pallas_call x1, Pallas kernels: 33.4 us -> 32.6 us  [local(): pl.pallas_call(kernel, out_shape=(pltpu.VMEM((1024, 128), F32), pltpu.VME...]
where the time goes in v4:
time: 33.6 us; the launch traced here: 33.5 us
  Pallas kernels  33.5 us (100%)
    pallas_call x1, Pallas kernels, local(): pl.pallas_call(kernel, out_shape=(pltpu.VMEM((1024, 128), F32), pltpu.VME...  32.6 us
    pallas_call x1, Pallas kernels, local(): pl.pallas_call(last, out_shape=jax.ShapeDtypeStruct((1024, 128), F32), in...  0.86 us

profile of v4, /device:TPU:1, one launch (start us, length us, event | category | flops | bytes accessed | tf_op | source)
XLA Modules:
  0.0 33.5 jit_solution(8387279196024450536)
XLA Ops:
  0.0 32.6 %shard_map.73 = (f32[1024,128]{1,0:T(8,128)S(1)}, bf16[1024,128]{1,0:T(8,128)(2,1)S(1)}) custom-call(f32[1024,128]{1,0:T(8,128)} %bitcast.23, bf16[64,64,128]{2,1,0:T(8,128)(2,1)} %bitcast.22, bf16[2,64,64,128]{3,2,1,0:T(8,128)(2,1)} %bitcast.21, s32[2,128]{1,0:T(2,128)} %bitcast.26, f32[1024,128]{1,0:T(8,128)} %bitcast.24, f32[4,2,64,64]{3,2,1,0:T(8,128)} %w_hbm.1, ...), custom_call_target="tpu_custom_call" | custom-call | flops 3000000000 | bytes 5000000 | tf_op jit(solution)/shard_map/pallas_call | solution.py:285
  32.6 0.9 %shard_map.74 = f32[1024,128]{1,0:T(8,128)} custom-call(f32[1024,128]{1,0:T(8,128)S(1)} %get-tuple-element.7.part, bf16[1024,128]{1,0:T(8,128)(2,1)S(1)} %get-tuple-element.8.cond), custom_call_target="tpu_custom_call" | custom-call | tf_op jit(solution)/shard_map/pallas_call | solution.py:332

commit v5 on v4

--- a/solution.py
+++ b/solution.py
@@ -33,8 +33,8 @@
 def kernel(
     sep_hbm, inv_hbm, couple_hbm, fidx_hbm, diag_hbm, w_hbm, sidx_hbm, out_v, cond_r,
     sep_v, inv_v, couple_v, fidx_v, diag_v, w_v, sidx_v,
-    rows_v, face_v, far_v, zrows_v, fidx_r, pick_s, pick_r, spread_s, spread_r, cond_v, cond_s,
-    driven_v, solved_v, sidx_t,
+    rows_v, face_v, turned_v, far_v, tables_v, zrows_v, fidx_r, pick_s, pick_r, spread_s, spread_r, cond_v, cond_s,
+    driven_v, solved_v, sidx_t, hot_v,
     in_sem, a_send, a_recv, i_send, i_recv, z_send, z_recv, c_send, c_recv, e_send, e_recv,
 ):
     s = lax.axis_index("sub")
@@ -72,6 +72,7 @@
             row = sep_v[pl.ds(l * 256 + c, 32, stride=8), :]
             rows_v[pl.ds((l * 8 + c) * 32, 32), :] = row
             face_v[pl.ds((l * 8 + c) * 32, 32), :] = row.astype(BF16)
+    turned_v[...] = jnp.transpose(rows_v[pl.ds((LEV - 1) * 256, 256), :]).astype(BF16)
     loads[1].wait()
 
     pl.semaphore_wait(barrier, LEV + NZP - 1)
@@ -83,7 +84,7 @@
         )
 
     def face_copy():
-        return to_partner(LEV - 1, face_v.at[pl.ds((LEV - 1) * 256, 256)], far_v, a_send, a_recv)
+        return to_partner(LEV - 1, turned_v, far_v, a_send, a_recv)
 
     def pick_copy(l):
         return to_partner(l, pick_s.at[l], pick_r.at[l], a_send, a_recv)
@@ -126,6 +127,8 @@
     picked = picked_from(face_v[pl.ds(0, 256), :], own_base[0], place)
     for l in range(1, LEV):
         picked += picked_from(face_v[pl.ds(l * 256, 256), :], own_base[l], place)
+    picked = jnp.where(odd, picked[BS:], picked[:BS])
+    tables_v[0] = one_hot(256, far_base, place)
     loads[2].wait()
     loads[3].wait()
     for l in (0, 1, 2):
@@ -135,14 +138,18 @@
         got = jnp.where(got_odd, got[BS:], got[:BS])
         pick_s[l] = jnp.concatenate([got[:, :NB], got[:, NB:]], axis=0).astype(BF16)
         pick_copy(l).start()
+    column = lax.broadcasted_iota(jnp.int32, (512, 512), 1)
+    picks = jnp.concatenate([sidx_t[pl.ds(e, 256, stride=2), :] for e in range(2)], axis=0)
+    for g in range(8):
+        hot_v[g] = jnp.where(column == picks[:, g : g + 1], 1.0, 0.0).astype(BF16)
     near = jnp.zeros((2 * BS, NB), F32)
     for l in (0, 1, 2):
         pick_copy(l).wait_recv()
         near += pick_r[l].astype(F32)
+    picked += jnp.concatenate([near[:BS], near[BS:]], axis=1)
     face_copy().wait_recv()
-    picked += picked_from(far_v[...], far_base, place)
-    picked = jnp.where(odd, picked[BS:], picked[:BS])
-    picked += jnp.concatenate([near[:BS], near[BS:]], axis=1)
+    far = jnp.dot(far_v[...], tables_v[0], preferred_element_type=F32)
+    picked += jnp.where(odd, far[BS:], far[:BS])
     first, second = picked[:, :NB], picked[:, NB:]
 
     def rows_of(i, body):
@@ -196,11 +203,13 @@
         if l == LEV - 1:
             idx_copy(l).wait_recv()
         got_odd, got_place = places(fidx_r[l])
+        if l == LEV - 1:
+            tables_v[1] = one_hot(256, own_base[l], got_place)
         spread_copy(l).wait_recv()
         values = spread_r[l].astype(F32)
         values = jnp.concatenate([values[:BS], values[BS:]], axis=1)
         values = halves_by_parity(values, got_odd).astype(BF16)
-        table = one_hot(256, own_base[l], got_place)
+        table = tables_v[1] if l == LEV - 1 else one_hot(256, own_base[l], got_place)
         part = cond_v[pl.ds(l * 256, 256), :] + lax.dot_general(
             table, values, NT, preferred_element_type=F32
         )
@@ -227,8 +236,6 @@
         weights += [left, left, right, right]
     w_high, w_low = split(jnp.concatenate(weights, axis=0))
     first_half = lax.broadcasted_iota(jnp.int32, (256, 128), 1) < BS
-    column = lax.broadcasted_iota(jnp.int32, (512, 512), 1)
-    picks = jnp.concatenate([sidx_t[pl.ds(e, 256, stride=2), :] for e in range(2)], axis=0)
 
     for peer in peers:
         z_copy(rows_v, zrows_v, peer, peer, peer, z_send, z_recv, peer).wait_recv()
@@ -240,7 +247,7 @@
         y += lax.dot_general(x_high, w_low, NT, preferred_element_type=F32)
         total = None
         for j in range(2):
-            table = jnp.where(column == picks[:, 2 * r + j : 2 * r + j + 1], 1.0, 0.0).astype(BF16)
+            table = hot_v[2 * r + j]
             parts = []
             for half in range(2):
                 g = 2 * j + half
@@ -297,7 +304,9 @@
             pltpu.VMEM((4, 2, 512), jnp.int32),
             pltpu.VMEM((1024, 128), F32),
             pltpu.VMEM((1024, 128), BF16),
-            pltpu.VMEM((256, 128), BF16),
+            pltpu.VMEM((128, 256), BF16),
+            pltpu.VMEM((128, 256), BF16),
+            pltpu.VMEM((2, 256, 256), BF16),
             pltpu.VMEM((1024, 128), F32),
             pltpu.VMEM((4, 2, 128), jnp.int32),
             pltpu.VMEM((3, 128, 128), BF16),
@@ -309,6 +318,7 @@
             pltpu.VMEM((64, 128), F32),
             pltpu.VMEM((64, 128), F32),
             pltpu.VMEM((512, 128), jnp.int32),
+            pltpu.VMEM((8, 512, 512), BF16),
             dma((7,)),
             dma((4,)),
             dma((4,)),

time: 33.6 us -> 33.6 us (level)
  no operation moved by 1% of the time
where the time goes in v5:
time: 33.6 us; the launch traced here: 33.5 us
  Pallas kernels  33.5 us (100%)
    pallas_call x1, Pallas kernels, local(): pl.pallas_call(kernel, out_shape=(pltpu.VMEM((1024, 128), F32), pltpu.VME...  32.6 us
    pallas_call x1, Pallas kernels, local(): pl.pallas_call(last, out_shape=jax.ShapeDtypeStruct((1024, 128), F32), in...  0.86 us

profile of v5, /device:TPU:1, one launch (start us, length us, event | category | flops | bytes accessed | tf_op | source)
XLA Modules:
  0.0 33.5 jit_solution(5461751246894934386)
XLA Ops:
  0.0 32.6 %shard_map.73 = (f32[1024,128]{1,0:T(8,128)S(1)}, bf16[1024,128]{1,0:T(8,128)(2,1)S(1)}) custom-call(f32[1024,128]{1,0:T(8,128)} %bitcast.23, bf16[64,64,128]{2,1,0:T(8,128)(2,1)} %bitcast.22, bf16[2,64,64,128]{3,2,1,0:T(8,128)(2,1)} %bitcast.21, s32[2,128]{1,0:T(2,128)} %bitcast.26, f32[1024,128]{1,0:T(8,128)} %bitcast.24, f32[4,2,64,64]{3,2,1,0:T(8,128)} %w_hbm.1, ...), custom_call_target="tpu_custom_call" | custom-call | flops 3000000000 | bytes 5000000 | tf_op jit(solution)/shard_map/pallas_call | solution.py:292
  32.6 0.9 %shard_map.74 = f32[1024,128]{1,0:T(8,128)} custom-call(f32[1024,128]{1,0:T(8,128)S(1)} %get-tuple-element.7.part, bf16[1024,128]{1,0:T(8,128)(2,1)S(1)} %get-tuple-element.8.cond), custom_call_target="tpu_custom_call" | custom-call | tf_op jit(solution)/shard_map/pallas_call | solution.py:342
